TPU v7x, 256 devices: a whole 4x4x8 slice. The times are simulated.
256 devices in a mesh: expert: 32 (over z, x), dp: 8 (over y, core).
Axes of the slice: x: 4, y: 4, z: 8, core: 2. Of those that a mesh axis runs over, the one named last changes fastest.
Arguments:
- tokens: bfloat16 [3072, 4096], P('expert', 'dp'), may hold values from -6 to 6
- route_weight: float32 [3072, 8], P('expert'), may hold values from 0.05 to 0.25
- route_expert: int32 [3072, 8], P('expert'), may hold values from 0 to 31, all different within a row; in each aligned block of 96 rows (0 to 95, 96 to 191, ...) at most 32 rows name the same one
- cotangent: bfloat16 [3072, 4096], P('expert', 'dp'), may hold values from -6 to 6
- gate_quant: bfloat16 [32, 4096, 1024], P('expert', None, 'dp'), may hold values from -0.09375 to 0.09375
- up_quant: bfloat16 [32, 4096, 1024], P('expert', None, 'dp'), may hold values from -0.09375 to 0.09375
- gate_scale: float32 [32, 32, 8], P('expert', None, 'dp'), may hold values from 0.5 to 2
- up_scale: float32 [32, 32, 8], P('expert', None, 'dp'), may hold values from 0.5 to 2
- down_quant: bfloat16 [32, 1024, 4096], P('expert', None, 'dp'), may hold values from -0.1875 to 0.1875
- down_scale: float32 [32, 8, 32], P('expert', None, 'dp'), may hold values from 0.5 to 2
- first_moment: float32 [32, 1024, 4096], P('expert', None, 'dp'), may hold values from -6 to 6
- second_moment: float32 [32, 1024, 4096], P('expert', None, 'dp'), may hold values from 0.5 to 8
- old_expert: int32 [32], replicated, may hold values from 0 to 31, each once
- new_holder: int32 [32], replicated, may hold values from 0 to 31, each once
Outputs:
- mixed: bfloat16 [3072, 4096], P('expert', 'dp')
- new_down: bfloat16 [32, 1024, 4096], P('expert', None, 'dp')
- new_first: float32 [32, 1024, 4096], P('expert', None, 'dp')
- new_second: float32 [32, 1024, 4096], P('expert', None, 'dp')
Inputs may be any that keep to these rules, and one draw needn't show every extreme that they name: `route_expert`: within each aligned block of 96 tokens (the tokens of one index of expert) no expert is named by more than 32 routes, a bound that some block reaches; a token names 8 different experts. `old_expert`: A permutation of the experts. `new_holder`: A permutation of the indices of expert.
All inputs are finite; a program needn't handle non-finite values.
Results may differ from a plain program's by a relative error of at most 0.0076.
Values may be sent and summed in bfloat16 or wider, within the bound.
A program may use at most 128 MiB of HBM per device.

v0:
```python
import jax
import jax.numpy as jnp
from jax import lax
from jax.sharding import PartitionSpec as P

QB = 128
beta_first = 0.9
beta_second = 0.95
adam_eps = 1e-08
learn_rate = 0.003
decay_rate = 0.1
step_count = 20


def dequantize(quant, scale):
    tiled = jnp.repeat(jnp.repeat(scale, QB, axis=0), QB, axis=1)
    return quant.astype(jnp.float32) * tiled


def adam_step(master, grad, first, second):
    first_new = beta_first * first + (1.0 - beta_first) * grad
    second_new = beta_second * second + (1.0 - beta_second) * grad * grad
    fix_first = 1.0 - beta_first**step_count
    fix_second = 1.0 - beta_second**step_count
    update = first_new / fix_first / (jnp.sqrt(second_new / fix_second) + adam_eps)
    fresh = (master - learn_rate * (update + decay_rate * master)).astype(jnp.bfloat16)
    return (fresh, first_new, second_new)


def holder_tables(old_expert, new_holder):
    number = old_expert.shape[0]
    labels = jnp.arange(number, dtype=jnp.int32)
    holds = (old_expert[:, None] == labels[None, :]).astype(jnp.int32)
    old_device = jnp.sum(holds * labels[:, None], axis=0)
    new_device = jnp.sum(holds * new_holder[:, None], axis=0)
    takes = (new_holder[:, None] == labels[None, :]).astype(jnp.int32)
    giver = jnp.sum(takes * labels[:, None], axis=0)
    return (old_device, new_device, giver)


def pack_rows(arrays, number):
    lines = []
    for array_item in arrays:
        line = array_item.reshape(-1)
        lines.append(line.reshape(number, -1))
    return jnp.concatenate(lines, axis=1)


def unpack_rows(packed, arrays):
    number = packed.shape[0]
    result = []
    offset = 0
    for array_item in arrays:
        span_cols = -(-array_item.size // number)
        block_rows = packed[:, offset : offset + span_cols]
        result.append(block_rows.reshape(-1).reshape(array_item.shape))
        offset = offset + span_cols
    return tuple(result)


def move_weights(arrays, giver):
    packed = pack_rows(arrays, giver.shape[0])
    spread = lax.all_to_all(packed, "expert", split_axis=0, concat_axis=0, tiled=True)
    settled = lax.all_to_all(
        jnp.take(spread, giver, axis=0), "expert", split_axis=0, concat_axis=0, tiled=True
    )
    return unpack_rows(settled, arrays)


def move_state(arrays, giver):
    packed = pack_rows(arrays, giver.shape[0])
    spread = lax.all_to_all(packed, "expert", split_axis=0, concat_axis=0, tiled=True)
    settled = lax.all_to_all(
        jnp.take(spread, giver, axis=0), "expert", split_axis=0, concat_axis=0, tiled=True
    )
    return unpack_rows(settled, arrays)


def plan_slots(route_expert, target_of, number, capacity):
    route_total = route_expert.shape[0] * route_expert.shape[1]
    flat_expert = route_expert.reshape(-1)
    labels = jnp.arange(number, dtype=jnp.int32)
    pick = (flat_expert[:, None] == labels[None, :]).astype(jnp.int32)
    target = jnp.sum(pick * target_of[None, :], axis=1)
    onehot = (target[:, None] == labels[None, :]).astype(jnp.int32)
    earlier = jnp.cumsum(onehot, axis=0) - onehot
    slot_index = jnp.sum(earlier * onehot, axis=1)
    route_place = target * capacity + slot_index
    slot_route = (
        jnp.full((number * capacity,), -1, jnp.int32)
        .at[route_place]
        .set(jnp.arange(route_total, dtype=jnp.int32))
    )
    return (route_place, slot_route)


def per_device(
    tokens,
    route_weight,
    route_expert,
    cotangent,
    gate_quant,
    up_quant,
    gate_scale,
    up_scale,
    down_quant,
    down_scale,
    first_moment,
    second_moment,
    old_expert,
    new_holder,
):
    number = lax.axis_size("expert")
    tok_rows, top_count = route_expert.shape
    model_width = gate_quant.shape[1]
    column_width = cotangent.shape[1]
    capacity = min(tok_rows, tok_rows * top_count // number * 4 // 3)
    old_device, new_device, giver = holder_tables(old_expert, new_holder)
    gate_quant, up_quant, down_quant = move_weights((gate_quant, up_quant, down_quant), giver)
    gate_scale, up_scale, down_scale, first_moment, second_moment = move_state(
        (gate_scale, up_scale, down_scale, first_moment, second_moment), giver
    )
    route_place, slot_route = plan_slots(route_expert, new_device, number, capacity)
    live_rows = slot_route >= 0
    safe_route = jnp.maximum(slot_route, 0)
    token_ids = safe_route // top_count
    weight_rows = jnp.where(
        live_rows, jnp.take(route_weight.reshape(-1), safe_route), jnp.float32(0.0)
    )
    back_rows = (
        weight_rows[:, None] * jnp.take(cotangent, token_ids, axis=0).astype(jnp.float32)
    ).astype(jnp.bfloat16)
    back_send = back_rows.reshape(number, capacity, column_width)
    whole_tokens = lax.all_gather(tokens, "dp", axis=1, tiled=True)
    sent_rows = jnp.take(whole_tokens, token_ids, axis=0).reshape(number, capacity, model_width)
    arrived, back_in = (
        lax.all_to_all(sent_rows, "expert", split_axis=0, concat_axis=0, tiled=True),
        lax.all_to_all(back_send, "expert", split_axis=0, concat_axis=0, tiled=True),
    )
    rows_in = arrived.reshape(-1, model_width)
    back_in = back_in.reshape(-1, column_width)
    gate_w = dequantize(gate_quant[0], gate_scale[0]).astype(jnp.bfloat16)
    up_w = dequantize(up_quant[0], up_scale[0]).astype(jnp.bfloat16)
    master = dequantize(down_quant[0], down_scale[0])
    down_w = master.astype(jnp.bfloat16)
    gate_val = jnp.dot(rows_in, gate_w, preferred_element_type=jnp.float32)
    up_val = jnp.dot(rows_in, up_w, preferred_element_type=jnp.float32)
    hidden_part = (jax.nn.silu(gate_val) * up_val).astype(jnp.bfloat16)
    hidden_full = lax.all_gather(hidden_part, "dp", axis=1, tiled=True)
    out_total = jnp.dot(hidden_full, down_w, preferred_element_type=jnp.float32)
    grad_total = lax.dot_general(
        hidden_full, back_in, (((0,), (0,)), ((), ())), preferred_element_type=jnp.float32
    )
    out_rows = out_total.astype(jnp.bfloat16).reshape(number, capacity, column_width)
    returned = lax.all_to_all(out_rows, "expert", split_axis=0, concat_axis=0, tiled=True).reshape(
        -1, column_width
    )
    picked = (
        jnp.take(returned, route_place, axis=0)
        .reshape(tok_rows, top_count, column_width)
        .astype(jnp.float32)
    )
    mixed = jnp.sum(picked * route_weight[:, :, None], axis=1).astype(jnp.bfloat16)
    fresh, first_new, second_new = adam_step(master, grad_total, first_moment[0], second_moment[0])
    fresh = fresh[None]
    first_new = first_new[None]
    second_new = second_new[None]
    return (mixed, fresh, first_new, second_new)


def solution(mesh):
    in_specs = (
        P("expert", "dp"),
        P("expert", None),
        P("expert", None),
        P("expert", "dp"),
        P("expert", None, "dp"),
        P("expert", None, "dp"),
        P("expert", None, "dp"),
        P("expert", None, "dp"),
        P("expert", None, "dp"),
        P("expert", None, "dp"),
        P("expert", None, "dp"),
        P("expert", None, "dp"),
        P(),
        P(),
    )
    out_specs = (
        P("expert", "dp"),
        P("expert", None, "dp"),
        P("expert", None, "dp"),
        P("expert", None, "dp"),
    )
    return jax.shard_map(
        per_device, mesh=mesh, in_specs=in_specs, out_specs=out_specs, check_vma=False
    )
```

profile of v0, /device:TPU:2, one launch (start us, length us, event | category | flops | bytes accessed | tf_op | source)
XLA Modules:
  0.0 698.2 jit_solution(656383670032208674)
XLA Ops:
  18.5 5.4 reshape.303
  23.9 11.8 %all-to-all-start.1 = ((bf16[32,2,24576]{2,1,0:T(2,128)(2,1)}), bf16[32,2,24576]{2,1,0:T(2,128)(2,1)S(1)}, u32[]{:S(2)}, u32[]{:S(2)}) async-start(bf16[32,2,24576]{2,1,0:T(2,128)(2,1)} %reshape.303), calls=%async_computation.1 | async-start | bytes 6291456 | tf_op jit(solution)/shard_map/all_to_all | solution.py:63
  45.6 9.3 %dynamic-update-slice.3 = f32[32,32771]{1,0:T(8,128)} dynamic-update-slice(f32[32,32771]{1,0:T(8,128)} %dynamic-update-slice.2, f32[32,16384]{1,0:T(8,128)} %reshape_reshape.30, s32[]{} %constant.150, s32[]{} %constant.153) | dynamic-update-slice | bytes 4194308
  54.9 8.7 %dynamic-update-slice.4 = f32[32,32771]{1,0:T(8,128)} dynamic-update-slice(f32[32,32771]{1,0:T(8,128)} %dynamic-update-slice.3, f32[32,16384]{1,0:T(8,128)} %reshape_reshape.31, s32[]{} %constant.150, s32[]{} %constant.154) | dynamic-update-slice | bytes 4194308 | tf_op jit(solution)/shard_map/concatenate | solution.py:46
  63.5 9.8 %all_to_all.43 = f32[32,1,32771]{2,1,0:T(1,128)} reshape(f32[32,32771]{1,0:T(8,128)} %dynamic-update-slice.4) | data formatting | bytes 8389376 | tf_op jit(solution)/shard_map/all_to_all | solution.py:72
  73.5 33.4 %all-to-all-done.1 = bf16[32,2,24576]{2,1,0:T(2,128)(2,1)S(1)} async-done(((bf16[32,2,24576]{2,1,0:T(2,128)(2,1)}), bf16[32,2,24576]{2,1,0:T(2,128)(2,1)S(1)}, u32[]{:S(2)}, u32[]{:S(2)}) %all-to-all-start.1) | async-done | bytes 3145760 | tf_op jit(solution)/shard_map/all_to_all | solution.py:63
  106.9 7.8 %all-to-all-start.3 = ((f32[32,1,32771]{2,1,0:T(1,128)}), f32[32,1,32771]{2,1,0:T(1,128)}, u32[]{:S(2)}, u32[]{:S(2)}) async-start(f32[32,1,32771]{2,1,0:T(1,128)} %all_to_all.43), calls=%async_computation.3 | async-start | bytes 8421376 | tf_op jit(solution)/shard_map/all_to_all | solution.py:72
  114.7 12.4 %reshape.304 = bf16[32,1,49152]{2,1,0:T(2,128)(2,1)} reshape(bf16[32,2,24576]{2,1,0:T(2,128)(2,1)S(1)} %all-to-all-done.1) | data formatting | bytes 6291456
  127.2 6.2 copy.83
  143.7 5.4 reshape.305
  149.1 59.0 %all-to-all-done.3 = f32[32,1,32771]{2,1,0:T(1,128)} async-done(((f32[32,1,32771]{2,1,0:T(1,128)}), f32[32,1,32771]{2,1,0:T(1,128)}, u32[]{:S(2)}, u32[]{:S(2)}) %all-to-all-start.3) | async-done | bytes 4194720 | tf_op jit(solution)/shard_map/all_to_all | solution.py:72
  208.1 8.3 %all-to-all-start.2 = ((bf16[32,2,24576]{2,1,0:T(2,128)(2,1)}), bf16[32,2,24576]{2,1,0:T(2,128)(2,1)}, u32[]{:S(2)}, u32[]{:S(2)}) async-start(bf16[32,2,24576]{2,1,0:T(2,128)(2,1)} %reshape.305), calls=%async_computation.2 | async-start | bytes 6291456 | tf_op jit(solution)/shard_map/all_to_all | solution.py:64
  220.9 7.6 %gather_fusion.2 = f32[32,32771]{1,0:T(8,128)} fusion(f32[32,32771]{1,0:T(8,128)} %bitcast.77, s32[1024]{0:T(1024)S(1)} %pad_clamp_fusion.1), kind=kCustom, calls=%fused_computation.2 | custom fusion | bytes 8389504 | tf_op jit(solution)/shard_map/jit(_take)/gather | solution.py:74
  231.0 6.3 copy.60
  237.3 50.3 %all-to-all-done.2 = bf16[32,2,24576]{2,1,0:T(2,128)(2,1)} async-done(((bf16[32,2,24576]{2,1,0:T(2,128)(2,1)}), bf16[32,2,24576]{2,1,0:T(2,128)(2,1)}, u32[]{:S(2)}, u32[]{:S(2)}) %all-to-all-start.2) | async-done | bytes 3145760 | tf_op jit(solution)/shard_map/all_to_all | solution.py:64
  287.6 7.4 %all-to-all-start.4 = ((f32[32,1,32771]{2,1,0:T(1,128)}), f32[32,1,32771]{2,1,0:T(1,128)}, u32[]{:S(2)}, u32[]{:S(2)}) async-start(f32[32,1,32771]{2,1,0:T(1,128)} %copy.60), calls=%async_computation.4 | async-start | bytes 8421376 | tf_op jit(solution)/shard_map/all_to_all | solution.py:73
  301.0 14.1 %all_gather.6 = bf16[96,4096]{1,0:T(8,128)(2,1)S(1)} all-gather(bf16[96,512]{1,0:T(8,128)(2,1)S(1)} %copy-done.7), channel_id=1, replica_groups=mesh['expert'=32,'dp'=8] {'dp'}, dimensions={1}, use_global_device_ids=true | all-gather | bytes 884736 | tf_op jit(solution)/shard_map/all_gather | solution.py:134
  315.1 7.8 %gather_fusion = bf16[1024,4096]{1,0:T(8,128)(2,1)} fusion(bf16[96,4096]{1,0:T(8,128)(2,1)S(1)} %all_gather.6, s32[1024]{0:T(1024)S(1)} %get-tuple-element.17), kind=kCustom, calls=%fused_computation | custom fusion | bytes 16781312 | tf_op jit(solution)/shard_map/jit(_take)/gather | solution.py:135
  322.9 7.4 %broadcast_select_fusion = bf16[32,32,4096]{2,1,0:T(8,128)(2,1)} fusion(bf16[32,32,4096]{2,1,0:T(8,128)(2,1)} %bitcast.80, pred[32,32]{1,0:T(8,128)(4,1)S(1)} %broadcast_in_dim.103), kind=kLoop, calls=%fused_computation.7 | loop fusion | flops 4194304 | bytes 16778240 | tf_op jit(solution)/shard_map/jit(_take)/select_n | solution.py:135
  330.3 58.3 %all-to-all-done.4 = f32[32,1,32771]{2,1,0:T(1,128)} async-done(((f32[32,1,32771]{2,1,0:T(1,128)}), f32[32,1,32771]{2,1,0:T(1,128)}, u32[]{:S(2)}, u32[]{:S(2)}) %all-to-all-start.4) | async-done | bytes 4194720 | tf_op jit(solution)/shard_map/all_to_all | solution.py:73
  388.7 7.7 %all-to-all-start = ((bf16[32,32,4096]{2,1,0:T(8,128)(2,1)}), bf16[32,32,4096]{2,1,0:T(8,128)(2,1)}, u32[]{:S(2)}, u32[]{:S(2)}) async-start(bf16[32,32,4096]{2,1,0:T(8,128)(2,1)} %broadcast_select_fusion), calls=%async_computation | async-start | bytes 16777216 | tf_op jit(solution)/shard_map/all_to_all | solution.py:137
  406.5 18.9 %reshape.306 = bf16[32,1,49152]{2,1,0:T(2,128)(2,1)} reshape(bf16[32,2,24576]{2,1,0:T(2,128)(2,1)} %all-to-all-done.2) | data formatting | bytes 6291456
  425.4 6.2 copy.82
  441.4 145.2 %all-to-all-done = bf16[32,32,4096]{2,1,0:T(8,128)(2,1)} async-done(((bf16[32,32,4096]{2,1,0:T(8,128)(2,1)}), bf16[32,32,4096]{2,1,0:T(8,128)(2,1)}, u32[]{:S(2)}, u32[]{:S(2)}) %all-to-all-start) | async-done | bytes 8388640 | tf_op jit(solution)/shard_map/all_to_all | solution.py:137
  586.6 13.2 %all-to-all-start.6 = ((bf16[32,32,512]{2,1,0:T(8,128)(2,1)}), bf16[32,32,512]{2,1,0:T(8,128)(2,1)}, u32[]{:S(2)}, u32[]{:S(2)}) async-start(bf16[32,32,512]{2,1,0:T(8,128)(2,1)} %multiply_convert_fusion), calls=%async_computation.6 | async-start | bytes 2097152 | tf_op jit(solution)/shard_map/all_to_all | solution.py:138
  600.1 6.0 fusion.15
  606.1 6.4 fusion.1
  615.9 27.8 %all-gather.2.cloned.1.call-done = bf16[1024,1024]{1,0:T(8,128)(2,1)} async-done(((bf16[1024,128]{1,0:T(8,128)(2,1)}), bf16[1024,1024]{1,0:T(8,128)(2,1)}) %all-gather.2.cloned.1.call-update) | async-done | bytes 2097168 | tf_op jit(solution)/shard_map/all_gather | solution.py:149
  648.5 10.1 %all-to-all-start.5 = ((bf16[32,32,512]{2,1,0:T(8,128)(2,1)}), bf16[32,32,512]{2,1,0:T(8,128)(2,1)S(1)}, u32[]{:S(2)}, u32[]{:S(2)}) async-start(bf16[32,32,512]{2,1,0:T(8,128)(2,1)} %bitcast.12), calls=%async_computation.5 | async-start | bytes 2097152 | tf_op jit(solution)/shard_map/all_to_all | solution.py:155
  658.7 4.7 slice_multiply_fusion
  667.6 9.3 %fusion.5 = (f32[1,1024,512]{2,1,0:T(8,128)}, bf16[1,1024,512]{2,1,0:T(8,128)(2,1)}, f32[1,1024,512]{2,1,0:T(8,128)}) fusion(f32[1024,512]{1,0:T(8,128)} %mul.146, f32[1024,512]{1,0:T(8,128)} %mul.139, f32[1024,512]{1,0:T(8,128)} %copy-done.3, f32[128,8,4,128]{3,2,1,0:T(4,128)} %bitcast.87, bf16[1024,1024]{1,0:T(8,128)(2,1)} %all-gather.2.cloned.1.call-done, ...), kind=kOutput, calls=%fused_computation.34 | convolution fusion | flops 1081606144 | bytes 16777216 | tf_op jit(solution)/shard_map/dot_general | solution.py:151
  676.9 10.2 %all-to-all-done.5 = bf16[32,32,512]{2,1,0:T(8,128)(2,1)S(1)} async-done(((bf16[32,32,512]{2,1,0:T(8,128)(2,1)}), bf16[32,32,512]{2,1,0:T(8,128)(2,1)S(1)}, u32[]{:S(2)}, u32[]{:S(2)}) %all-to-all-start.5) | async-done | bytes 1048608 | tf_op jit(solution)/shard_map/all_to_all | solution.py:155
  (100 shorter events, 81.0 us)
Async XLA Ops:
  7.2 394.1 %copy-start = (bf16[96,512]{1,0:T(8,128)(2,1)S(1)}, bf16[96,512]{1,0:T(8,128)(2,1)}, u32[]{:S(2)}) copy-start(bf16[96,512]{1,0:T(8,128)(2,1)} %param.17) | copy-start | bytes 294916
  7.2 2.5 copy-start.4
  7.2 3.7 copy-start.5
  23.9 11.8 %copy-start.11 = (f32[1,32,1]{1,2,0:T(1,128)S(1)}, f32[1,32,1]{1,2,0:T(1,128)}, u32[]{:S(2)}) copy-start(f32[1,32,1]{1,2,0:T(1,128)} %param.20) | copy-start | bytes 388
  23.9 11.9 %copy-start.12 = (f32[1,32,1]{1,2,0:T(1,128)S(1)}, f32[1,32,1]{1,2,0:T(1,128)}, u32[]{:S(2)}) copy-start(f32[1,32,1]{1,2,0:T(1,128)} %param.21) | copy-start | bytes 388
  23.9 12.0 %copy-start.10 = (f32[1,8,4]{1,2,0:T(4,128)S(1)}, f32[1,8,4]{1,2,0:T(4,128)}, u32[]{:S(2)}) copy-start(f32[1,8,4]{1,2,0:T(4,128)} %param.23) | copy-start | bytes 388
  23.9 83.0 %all-to-all-start.1 = ((bf16[32,2,24576]{2,1,0:T(2,128)(2,1)}), bf16[32,2,24576]{2,1,0:T(2,128)(2,1)S(1)}, u32[]{:S(2)}, u32[]{:S(2)}) async-start(bf16[32,2,24576]{2,1,0:T(2,128)(2,1)} %reshape.303), calls=%async_computation.1 | async-start | bytes 6291456 | tf_op jit(solution)/shard_map/all_to_all | solution.py:63
  63.5 9.8 %copy-start.13 = (s32[32]{0:T(128)S(1)}, s32[32]{0:T(128)}, u32[]{:S(2)}) copy-start(s32[32]{0:T(128)} %param.27) | copy-start | bytes 388
  63.5 9.8 %copy-start.14 = (s32[32]{0:T(128)S(1)}, s32[32]{0:T(128)}, u32[]{:S(2)}) copy-start(s32[32]{0:T(128)} %param.26) | copy-start | bytes 388
  106.9 101.2 %all-to-all-start.3 = ((f32[32,1,32771]{2,1,0:T(1,128)}), f32[32,1,32771]{2,1,0:T(1,128)}, u32[]{:S(2)}, u32[]{:S(2)}) async-start(f32[32,1,32771]{2,1,0:T(1,128)} %all_to_all.43), calls=%async_computation.3 | async-start | bytes 8421376 | tf_op jit(solution)/shard_map/all_to_all | solution.py:72
  208.1 79.5 %all-to-all-start.2 = ((bf16[32,2,24576]{2,1,0:T(2,128)(2,1)}), bf16[32,2,24576]{2,1,0:T(2,128)(2,1)}, u32[]{:S(2)}, u32[]{:S(2)}) async-start(bf16[32,2,24576]{2,1,0:T(2,128)(2,1)} %reshape.305), calls=%async_computation.2 | async-start | bytes 6291456 | tf_op jit(solution)/shard_map/all_to_all | solution.py:64
  237.3 57.7 %copy-start.8 = (s32[96,8]{0,1:T(8,128)S(1)}, s32[96,8]{0,1:T(8,128)}, u32[]{:S(2)}) copy-start(s32[96,8]{0,1:T(8,128)} %param.16) | copy-start | bytes 9220
  237.3 63.7 %copy-start.7 = (bf16[96,512]{1,0:T(8,128)(2,1)S(1)}, bf16[96,512]{1,0:T(8,128)(2,1)}, u32[]{:S(2)}) copy-start(bf16[96,512]{1,0:T(8,128)(2,1)} %param.14) | copy-start | bytes 294916
  287.6 101.0 %all-to-all-start.4 = ((f32[32,1,32771]{2,1,0:T(1,128)}), f32[32,1,32771]{2,1,0:T(1,128)}, u32[]{:S(2)}, u32[]{:S(2)}) async-start(f32[32,1,32771]{2,1,0:T(1,128)} %copy.60), calls=%async_computation.4 | async-start | bytes 8421376 | tf_op jit(solution)/shard_map/all_to_all | solution.py:73
  330.3 66.1 %copy-start.9 = (f32[96,8]{0,1:T(8,128)S(1)}, f32[96,8]{0,1:T(8,128)}, u32[]{:S(2)}) copy-start(f32[96,8]{0,1:T(8,128)} %param.15) | copy-start | bytes 9220
  388.7 198.0 %all-to-all-start = ((bf16[32,32,4096]{2,1,0:T(8,128)(2,1)}), bf16[32,32,4096]{2,1,0:T(8,128)(2,1)}, u32[]{:S(2)}, u32[]{:S(2)}) async-start(bf16[32,32,4096]{2,1,0:T(8,128)(2,1)} %broadcast_select_fusion), calls=%async_computation | async-start | bytes 16777216 | tf_op jit(solution)/shard_map/all_to_all | solution.py:137
  434.1 2.6 copy-start.1
  586.6 61.9 %all-to-all-start.6 = ((bf16[32,32,512]{2,1,0:T(8,128)(2,1)}), bf16[32,32,512]{2,1,0:T(8,128)(2,1)}, u32[]{:S(2)}, u32[]{:S(2)}) async-start(bf16[32,32,512]{2,1,0:T(8,128)(2,1)} %multiply_convert_fusion), calls=%async_computation.6 | async-start | bytes 2097152 | tf_op jit(solution)/shard_map/all_to_all | solution.py:138
  599.8 43.9 %all-gather.2.cloned.1.call-start = ((), (), s32[]{:S(2)}) async-start(), calls=%async_computation.7 | async-start | bytes 2359296 | tf_op jit(solution)/shard_map/all_gather | solution.py:149
  600.1 6.0 copy-start.6
  615.8 32.8 %copy-start.3 = (f32[1024,512]{1,0:T(8,128)}, f32[1024,512]{1,0:T(8,128)S(1)}, u32[]{:S(2)}) copy-start(f32[1024,512]{1,0:T(8,128)S(1)} %reshape.234) | copy-start | bytes 6291460
  643.6 2.6 copy-start.15
  644.9 1.3 copy-start.2
  648.5 38.6 %all-to-all-start.5 = ((bf16[32,32,512]{2,1,0:T(8,128)(2,1)}), bf16[32,32,512]{2,1,0:T(8,128)(2,1)S(1)}, u32[]{:S(2)}, u32[]{:S(2)}) async-start(bf16[32,32,512]{2,1,0:T(8,128)(2,1)} %bitcast.12), calls=%async_computation.5 | async-start | bytes 2097152 | tf_op jit(solution)/shard_map/all_to_all | solution.py:155
Sparse Core Ops, SparseCore 0:
  612.7 30.9 all-gather.1
where the time goes:
time: 706 us; the launch traced here: 698 us
  waiting for transfers between devices  384 us (54%)
  local copies, waits for them, and re-layouts  160 us (23%)
  starting transfers between devices  66.5 us (9%)
  other arithmetic  34.7 us (5%)
  matrix products  24 us (3%)
  between operations  14.6 us (2%)
  blocking collectives  14.1 us (2%)
    all_to_all x1, waiting for transfers between devices, per_device(): lax.all_to_all(sent_rows, 'expert', split_axis=0, concat_axis=0, tiled=True)  145 us
    unnamed x47, local copies, waits for them, and re-layouts  76.8 us
    all_to_all x1, waiting for transfers between devices, move_state(): lax.all_to_all(packed, 'expert', split_axis=0, concat_axis=0, tiled=True)  59 us
    all_to_all x1, waiting for transfers between devices, move_state(): lax.all_to_all(jnp.take(spread, giver, axis=0), 'expert', split_axis=0, c...  58.3 us
    all_to_all x1, waiting for transfers between devices, move_weights(): lax.all_to_all(jnp.take(spread, giver, axis=0), 'expert', split_axis=0, c...  50.3 us
    all_to_all x1, waiting for transfers between devices, move_weights(): lax.all_to_all(packed, 'expert', split_axis=0, concat_axis=0, tiled=True)  33.4 us
    all_gather x1, waiting for transfers between devices, per_device(): hidden_full = lax.all_gather(hidden_part, 'dp', axis=1, tiled=True)  27.8 us
  transfers between devices with their start and end apart: 8, of which 7 were waited for; matrix products, arithmetic and copies ran while one was open for 27% of the time, Pallas kernels for 0%

commit v1 on v0

--- a/solution.py
+++ b/solution.py
@@ -10,6 +10,12 @@
 learn_rate = 0.003
 decay_rate = 0.1
 step_count = 20
+
+
+def fix_things(sample, pos_dim):
+    mixed_arr = list(sample.shape[1:])
+    mixed_arr[pos_dim] *= sample.shape[0]
+    return jnp.moveaxis(sample, 0, pos_dim).reshape(mixed_arr)
 
 
 def dequantize(quant, scale):
@@ -146,7 +152,23 @@
     gate_val = jnp.dot(rows_in, gate_w, preferred_element_type=jnp.float32)
     up_val = jnp.dot(rows_in, up_w, preferred_element_type=jnp.float32)
     hidden_part = (jax.nn.silu(gate_val) * up_val).astype(jnp.bfloat16)
-    hidden_full = lax.all_gather(hidden_part, "dp", axis=1, tiled=True)
+    cores_n = lax.axis_size("dp")
+    fields = tuple(((idx, (idx + 1) % cores_n) for idx in range(cores_n)))
+    y2, value_now = ([], [])
+    line_up = tuple(((k0, s) for s, k0 in fields))
+    for c in range(cores_n - 1):
+        if c % 2 == 0:
+            y2.append(lax.ppermute(y2[-1] if y2 else hidden_part, "dp", fields))
+        else:
+            value_now.append(
+                lax.ppermute(value_now[-1] if value_now else hidden_part, "dp", line_up)
+            )
+    reply = jnp.stack([*y2[::-1], hidden_part, *value_now], axis=0)
+    known = len(y2)
+    view_out = lax.axis_index("dp")
+    piece_next = view_out - known
+    reply = reply[(jnp.arange(cores_n) - piece_next) % cores_n]
+    hidden_full = fix_things(reply, 1)
     out_total = jnp.dot(hidden_full, down_w, preferred_element_type=jnp.float32)
     grad_total = lax.dot_general(
         hidden_full, back_in, (((0,), (0,)), ((), ())), preferred_element_type=jnp.float32

time: 706 us -> 693 us (0.982)
  waiting for transfers between devices: 384 us -> 358 us
  local copies, waits for them, and re-layouts: 160 us -> 176 us
  between operations: 14.6 us -> 1.35 us
  starting transfers between devices: 66.5 us -> 75.1 us
    all_gather x1 -> x0, waiting for transfers between devices: 27.8 us -> none  [per_device(): hidden_full = lax.all_gather(hidden_part, 'dp', axis=1, tiled=True)]
    ppermute x0 -> x7, starting transfers between devices: none -> 9.26 us  [the longest x3 8.14 us: per_device(): lax.ppermute(value_now[-1] if value_now else hidden_part, 'dp', line_up)]
    unnamed x47 -> x84, local copies, waits for them, and re-layouts: 76.8 us -> 84.2 us
  transfers between devices with their start and end apart: 8 -> 14, of which waited for: 7 -> 8; matrix products, arithmetic and copies ran while one was open for 27% -> 28% of each run, Pallas kernels for 0% -> 0%
where the time goes in v1:
time: 693 us; the launch traced here: 686 us
  waiting for transfers between devices  358 us (52%)
  local copies, waits for them, and re-layouts  176 us (25%)
  starting transfers between devices  75.1 us (11%)
  other arithmetic  37.5 us (5%)
  matrix products  23.5 us (3%)
  blocking collectives  14.3 us (2%)
    all_to_all x1, waiting for transfers between devices, per_device(): lax.all_to_all(sent_rows, 'expert', split_axis=0, concat_axis=0, tiled=True)  148 us
    unnamed x84, local copies, waits for them, and re-layouts  84.2 us
    all_to_all x1, waiting for transfers between devices, move_state(): lax.all_to_all(packed, 'expert', split_axis=0, concat_axis=0, tiled=True)  58.9 us
    all_to_all x1, waiting for transfers between devices, move_state(): lax.all_to_all(jnp.take(spread, giver, axis=0), 'expert', split_axis=0, c...  58.1 us
    all_to_all x1, waiting for transfers between devices, move_weights(): lax.all_to_all(jnp.take(spread, giver, axis=0), 'expert', split_axis=0, c...  50.3 us
    all_to_all x1, waiting for transfers between devices, move_weights(): lax.all_to_all(packed, 'expert', split_axis=0, concat_axis=0, tiled=True)  33.4 us
    all_gather x1, blocking collectives, per_device(): whole_tokens = lax.all_gather(tokens, 'dp', axis=1, tiled=True)  14.3 us
  transfers between devices with their start and end apart: 14, of which 8 were waited for; matrix products, arithmetic and copies ran while one was open for 28% of the time, Pallas kernels for 0%

profile of v1, /device:TPU:2, one launch (start us, length us, event | category | flops | bytes accessed | tf_op | source)
XLA Modules:
  0.0 685.8 jit_solution(148616743044260505)
XLA Ops:
  11.9 5.4 reshape.381
  17.3 11.8 %all-to-all-start.1 = ((bf16[32,2,24576]{2,1,0:T(2,128)(2,1)}), bf16[32,2,24576]{2,1,0:T(2,128)(2,1)S(1)}, u32[]{:S(2)}, u32[]{:S(2)}) async-start(bf16[32,2,24576]{2,1,0:T(2,128)(2,1)} %reshape.381), calls=%async_computation.1 | async-start | bytes 6291456 | tf_op jit(solution)/shard_map/all_to_all | solution.py:69
  39.0 9.3 %dynamic-update-slice.11 = f32[32,32771]{1,0:T(8,128)} dynamic-update-slice(f32[32,32771]{1,0:T(8,128)} %dynamic-update-slice.10, f32[32,16384]{1,0:T(8,128)} %reshape_reshape.30, s32[]{} %constant.171, s32[]{} %constant.174) | dynamic-update-slice | bytes 4194308
  48.3 8.7 %dynamic-update-slice.12 = f32[32,32771]{1,0:T(8,128)} dynamic-update-slice(f32[32,32771]{1,0:T(8,128)} %dynamic-update-slice.11, f32[32,16384]{1,0:T(8,128)} %reshape_reshape.31, s32[]{} %constant.171, s32[]{} %constant.179) | dynamic-update-slice | bytes 4194308 | tf_op jit(solution)/shard_map/concatenate | solution.py:52
  57.0 9.8 %all_to_all.43 = f32[32,1,32771]{2,1,0:T(1,128)} reshape(f32[32,32771]{1,0:T(8,128)} %dynamic-update-slice.12) | data formatting | bytes 8389376 | tf_op jit(solution)/shard_map/all_to_all | solution.py:78
  66.9 33.4 %all-to-all-done.1 = bf16[32,2,24576]{2,1,0:T(2,128)(2,1)S(1)} async-done(((bf16[32,2,24576]{2,1,0:T(2,128)(2,1)}), bf16[32,2,24576]{2,1,0:T(2,128)(2,1)S(1)}, u32[]{:S(2)}, u32[]{:S(2)}) %all-to-all-start.1) | async-done | bytes 3145760 | tf_op jit(solution)/shard_map/all_to_all | solution.py:69
  100.3 7.7 %all-to-all-start.3 = ((f32[32,1,32771]{2,1,0:T(1,128)}), f32[32,1,32771]{2,1,0:T(1,128)}, u32[]{:S(2)}, u32[]{:S(2)}) async-start(f32[32,1,32771]{2,1,0:T(1,128)} %all_to_all.43), calls=%async_computation.3 | async-start | bytes 8421376 | tf_op jit(solution)/shard_map/all_to_all | solution.py:78
  108.0 12.5 %reshape.382 = bf16[32,1,49152]{2,1,0:T(2,128)(2,1)} reshape(bf16[32,2,24576]{2,1,0:T(2,128)(2,1)S(1)} %all-to-all-done.1) | data formatting | bytes 6291456
  120.6 6.2 copy.91
  137.1 5.4 reshape.383
  142.5 58.9 %all-to-all-done.3 = f32[32,1,32771]{2,1,0:T(1,128)} async-done(((f32[32,1,32771]{2,1,0:T(1,128)}), f32[32,1,32771]{2,1,0:T(1,128)}, u32[]{:S(2)}, u32[]{:S(2)}) %all-to-all-start.3) | async-done | bytes 4194720 | tf_op jit(solution)/shard_map/all_to_all | solution.py:78
  201.4 8.0 %all-to-all-start.2 = ((bf16[32,2,24576]{2,1,0:T(2,128)(2,1)}), bf16[32,2,24576]{2,1,0:T(2,128)(2,1)}, u32[]{:S(2)}, u32[]{:S(2)}) async-start(bf16[32,2,24576]{2,1,0:T(2,128)(2,1)} %reshape.383), calls=%async_computation.2 | async-start | bytes 6291456 | tf_op jit(solution)/shard_map/all_to_all | solution.py:70
  213.9 7.7 %gather_fusion.2 = f32[32,32771]{1,0:T(8,128)} fusion(f32[32,32771]{1,0:T(8,128)} %bitcast.100, s32[1024]{0:T(1024)S(1)} %pad_clamp_fusion.2), kind=kCustom, calls=%fused_computation.2 | custom fusion | bytes 8389504 | tf_op jit(solution)/shard_map/jit(_take)/gather | solution.py:80
  224.1 6.3 copy.63
  230.4 50.3 %all-to-all-done.2 = bf16[32,2,24576]{2,1,0:T(2,128)(2,1)} async-done(((bf16[32,2,24576]{2,1,0:T(2,128)(2,1)}), bf16[32,2,24576]{2,1,0:T(2,128)(2,1)}, u32[]{:S(2)}, u32[]{:S(2)}) %all-to-all-start.2) | async-done | bytes 3145760 | tf_op jit(solution)/shard_map/all_to_all | solution.py:70
  280.6 7.4 %all-to-all-start.4 = ((f32[32,1,32771]{2,1,0:T(1,128)}), f32[32,1,32771]{2,1,0:T(1,128)}, u32[]{:S(2)}, u32[]{:S(2)}) async-start(f32[32,1,32771]{2,1,0:T(1,128)} %copy.63), calls=%async_computation.4 | async-start | bytes 8421376 | tf_op jit(solution)/shard_map/all_to_all | solution.py:79
  294.0 14.3 %all_gather.3 = bf16[96,4096]{1,0:T(8,128)(2,1)S(1)} all-gather(bf16[96,512]{1,0:T(8,128)(2,1)S(1)} %copy-done.13), channel_id=1, replica_groups=mesh['expert'=32,'dp'=8] {'dp'}, dimensions={1}, use_global_device_ids=true | all-gather | bytes 884736 | tf_op jit(solution)/shard_map/all_gather | solution.py:140
  308.4 7.8 %gather_fusion = bf16[1024,4096]{1,0:T(8,128)(2,1)} fusion(bf16[96,4096]{1,0:T(8,128)(2,1)S(1)} %all_gather.3, s32[1024]{0:T(1024)S(1)} %get-tuple-element.17), kind=kCustom, calls=%fused_computation | custom fusion | bytes 16781312 | tf_op jit(solution)/shard_map/jit(_take)/gather | solution.py:141
  316.2 7.4 %broadcast_select_fusion = bf16[32,32,4096]{2,1,0:T(8,128)(2,1)} fusion(bf16[32,32,4096]{2,1,0:T(8,128)(2,1)} %bitcast.103, pred[32,32]{1,0:T(8,128)(4,1)S(1)} %broadcast_in_dim.104), kind=kLoop, calls=%fused_computation.8 | loop fusion | flops 4194304 | bytes 16778240 | tf_op jit(solution)/shard_map/jit(_take)/select_n | solution.py:141
  323.6 58.1 %all-to-all-done.4 = f32[32,1,32771]{2,1,0:T(1,128)} async-done(((f32[32,1,32771]{2,1,0:T(1,128)}), f32[32,1,32771]{2,1,0:T(1,128)}, u32[]{:S(2)}, u32[]{:S(2)}) %all-to-all-start.4) | async-done | bytes 4194720 | tf_op jit(solution)/shard_map/all_to_all | solution.py:79
  381.6 7.6 %all-to-all-start = ((bf16[32,32,4096]{2,1,0:T(8,128)(2,1)}), bf16[32,32,4096]{2,1,0:T(8,128)(2,1)}, u32[]{:S(2)}, u32[]{:S(2)}) async-start(bf16[32,32,4096]{2,1,0:T(8,128)(2,1)} %broadcast_select_fusion), calls=%async_computation | async-start | bytes 16777216 | tf_op jit(solution)/shard_map/all_to_all | solution.py:143
  389.5 4.5 gather_fusion.5
  398.7 19.0 %reshape.384 = bf16[32,1,49152]{2,1,0:T(2,128)(2,1)} reshape(bf16[32,2,24576]{2,1,0:T(2,128)(2,1)} %all-to-all-done.2) | data formatting | bytes 6291456
  417.7 6.2 copy.90
  432.0 147.6 %all-to-all-done = bf16[32,32,4096]{2,1,0:T(8,128)(2,1)} async-done(((bf16[32,32,4096]{2,1,0:T(8,128)(2,1)}), bf16[32,32,4096]{2,1,0:T(8,128)(2,1)}, u32[]{:S(2)}, u32[]{:S(2)}) %all-to-all-start) | async-done | bytes 8388640 | tf_op jit(solution)/shard_map/all_to_all | solution.py:143
  579.6 5.8 fusion.18
  585.4 5.7 fusion.1
  592.6 13.5 %all-to-all-start.6 = ((bf16[32,32,512]{2,1,0:T(8,128)(2,1)}), bf16[32,32,512]{2,1,0:T(8,128)(2,1)}, u32[]{:S(2)}, u32[]{:S(2)}) async-start(bf16[32,32,512]{2,1,0:T(8,128)(2,1)} %multiply_convert_fusion), calls=%async_computation.6 | async-start | bytes 2097152 | tf_op jit(solution)/shard_map/all_to_all | solution.py:144
  646.5 9.8 %all-to-all-start.5 = ((bf16[32,32,512]{2,1,0:T(8,128)(2,1)}), bf16[32,32,512]{2,1,0:T(8,128)(2,1)S(1)}, u32[]{:S(2)}, u32[]{:S(2)}) async-start(bf16[32,32,512]{2,1,0:T(8,128)(2,1)} %bitcast.23), calls=%async_computation.5 | async-start | bytes 2097152 | tf_op jit(solution)/shard_map/all_to_all | solution.py:177
  656.3 4.7 slice_multiply_fusion
  667.6 8.1 %fusion.6 = (f32[1,1024,512]{2,1,0:T(8,128)}, bf16[1,1024,512]{2,1,0:T(8,128)(2,1)}, f32[1,1024,512]{2,1,0:T(8,128)}) fusion(f32[1024,512]{1,0:T(8,128)} %mul.156, f32[1024,512]{1,0:T(8,128)} %mul.149, f32[1024,512]{1,0:T(8,128)S(1)} %copy-done.4, f32[128,8,4,128]{3,2,1,0:T(4,128)S(1)} %bitcast.112, bf16[1024,1024]{0,1:T(8,128)(2,1)} %bitcast.114, ...), kind=kOutput, calls=%fused_computation.37 | convolution fusion | flops 1081606144 | bytes 16777216 | tf_op jit(solution)/shard_map/dot_general | solution.py:173
  675.7 5.9 all-to-all-done.5
  (155 shorter events, 109.6 us)
Async XLA Ops:
  0.6 394.1 %copy-start = (bf16[96,512]{1,0:T(8,128)(2,1)S(1)}, bf16[96,512]{1,0:T(8,128)(2,1)}, u32[]{:S(2)}) copy-start(bf16[96,512]{1,0:T(8,128)(2,1)} %param.17) | copy-start | bytes 294916
  17.3 11.8 %copy-start.27 = (f32[1,32,1]{1,2,0:T(1,128)S(1)}, f32[1,32,1]{1,2,0:T(1,128)}, u32[]{:S(2)}) copy-start(f32[1,32,1]{1,2,0:T(1,128)} %param.20) | copy-start | bytes 388
  17.3 11.9 %copy-start.28 = (f32[1,32,1]{1,2,0:T(1,128)S(1)}, f32[1,32,1]{1,2,0:T(1,128)}, u32[]{:S(2)}) copy-start(f32[1,32,1]{1,2,0:T(1,128)} %param.21) | copy-start | bytes 388
  17.3 12.0 %copy-start.26 = (f32[1,8,4]{1,2,0:T(4,128)S(1)}, f32[1,8,4]{1,2,0:T(4,128)}, u32[]{:S(2)}) copy-start(f32[1,8,4]{1,2,0:T(4,128)} %param.23) | copy-start | bytes 388
  17.3 83.0 %all-to-all-start.1 = ((bf16[32,2,24576]{2,1,0:T(2,128)(2,1)}), bf16[32,2,24576]{2,1,0:T(2,128)(2,1)S(1)}, u32[]{:S(2)}, u32[]{:S(2)}) async-start(bf16[32,2,24576]{2,1,0:T(2,128)(2,1)} %reshape.381), calls=%async_computation.1 | async-start | bytes 6291456 | tf_op jit(solution)/shard_map/all_to_all | solution.py:69
  57.0 9.8 %copy-start.29 = (s32[32]{0:T(128)S(1)}, s32[32]{0:T(128)}, u32[]{:S(2)}) copy-start(s32[32]{0:T(128)} %param.27) | copy-start | bytes 388
  57.0 9.8 %copy-start.30 = (s32[32]{0:T(128)S(1)}, s32[32]{0:T(128)}, u32[]{:S(2)}) copy-start(s32[32]{0:T(128)} %param.26) | copy-start | bytes 388
  100.3 101.1 %all-to-all-start.3 = ((f32[32,1,32771]{2,1,0:T(1,128)}), f32[32,1,32771]{2,1,0:T(1,128)}, u32[]{:S(2)}, u32[]{:S(2)}) async-start(f32[32,1,32771]{2,1,0:T(1,128)} %all_to_all.43), calls=%async_computation.3 | async-start | bytes 8421376 | tf_op jit(solution)/shard_map/all_to_all | solution.py:78
  201.4 79.2 %all-to-all-start.2 = ((bf16[32,2,24576]{2,1,0:T(2,128)(2,1)}), bf16[32,2,24576]{2,1,0:T(2,128)(2,1)}, u32[]{:S(2)}, u32[]{:S(2)}) async-start(bf16[32,2,24576]{2,1,0:T(2,128)(2,1)} %reshape.383), calls=%async_computation.2 | async-start | bytes 6291456 | tf_op jit(solution)/shard_map/all_to_all | solution.py:70
  230.4 57.6 %copy-start.23 = (s32[96,8]{0,1:T(8,128)S(1)}, s32[96,8]{0,1:T(8,128)}, u32[]{:S(2)}) copy-start(s32[96,8]{0,1:T(8,128)} %param.16) | copy-start | bytes 9220
  230.4 63.7 %copy-start.13 = (bf16[96,512]{1,0:T(8,128)(2,1)S(1)}, bf16[96,512]{1,0:T(8,128)(2,1)}, u32[]{:S(2)}) copy-start(bf16[96,512]{1,0:T(8,128)(2,1)} %param.14) | copy-start | bytes 294916
  280.6 101.0 %all-to-all-start.4 = ((f32[32,1,32771]{2,1,0:T(1,128)}), f32[32,1,32771]{2,1,0:T(1,128)}, u32[]{:S(2)}, u32[]{:S(2)}) async-start(f32[32,1,32771]{2,1,0:T(1,128)} %copy.63), calls=%async_computation.4 | async-start | bytes 8421376 | tf_op jit(solution)/shard_map/all_to_all | solution.py:79
  294.0 22.1 %copy-start.16 = (pred[32,32]{1,0:T(8,128)(4,1)}, pred[32,32]{1,0:T(8,128)(4,1)S(1)}, u32[]{:S(2)}) copy-start(pred[32,32]{1,0:T(8,128)(4,1)S(1)} %broadcast_in_dim.104) | copy-start | bytes 3076
  323.6 65.7 %copy-start.24 = (f32[96,8]{0,1:T(8,128)S(1)}, f32[96,8]{0,1:T(8,128)}, u32[]{:S(2)}) copy-start(f32[96,8]{0,1:T(8,128)} %param.15) | copy-start | bytes 9220
  381.6 198.0 %all-to-all-start = ((bf16[32,32,4096]{2,1,0:T(8,128)(2,1)}), bf16[32,32,4096]{2,1,0:T(8,128)(2,1)}, u32[]{:S(2)}, u32[]{:S(2)}) async-start(bf16[32,32,4096]{2,1,0:T(8,128)(2,1)} %broadcast_select_fusion), calls=%async_computation | async-start | bytes 16777216 | tf_op jit(solution)/shard_map/all_to_all | solution.py:143
  430.7 148.9 %copy-start.7 = (bf16[4096,128]{1,0:T(8,128)(2,1)S(1)}, bf16[4096,128]{1,0:T(8,128)(2,1)}, u32[]{:S(2)}) copy-start(bf16[4096,128]{1,0:T(8,128)(2,1)} %convert_element_type.87) | copy-start | bytes 3145732
  591.1 15.6 %collective-permute-start = (bf16[1024,128]{1,0:T(8,128)(2,1)S(1)}, bf16[1024,128]{1,0:T(8,128)(2,1)S(1)}, u32[]{:S(2)}, u32[]{:S(2)}) collective-permute-start(bf16[1024,128]{1,0:T(8,128)(2,1)S(1)} %fusion.1), channel_id=1, source_target_pairs={{0,1},{1,2},{2,3},{3,4},{4,5},{5,6},{6,7},{7,0},{8,9},{9,10},{10,1... | collective-permute-start | bytes 786440 | tf_op jit(solution)/shard_map/ppermute | solution.py:161
  591.2 14.9 %copy-start.22 = (s32[768]{0:T(1024)S(1)}, s32[768]{0:T(1024)}, u32[]{:S(2)}) copy-start(s32[768]{0:T(1024)} %copy-done.21) | copy-start | bytes 9220
  591.2 17.2 %copy-start.19 = (s32[768]{0:T(1024)S(1)}, s32[768]{0:T(1024)}, u32[]{:S(2)}) copy-start(s32[768]{0:T(1024)} %copy-done.18) | copy-start | bytes 9220
  592.6 54.0 %all-to-all-start.6 = ((bf16[32,32,512]{2,1,0:T(8,128)(2,1)}), bf16[32,32,512]{2,1,0:T(8,128)(2,1)}, u32[]{:S(2)}, u32[]{:S(2)}) async-start(bf16[32,32,512]{2,1,0:T(8,128)(2,1)} %multiply_convert_fusion), calls=%async_computation.6 | async-start | bytes 2097152 | tf_op jit(solution)/shard_map/all_to_all | solution.py:144
  606.7 7.0 %copy-start.9 = (bf16[1024,128]{1,0:T(8,128)(2,1)}, bf16[1024,128]{1,0:T(8,128)(2,1)S(1)}, u32[]{:S(2)}) copy-start(bf16[1024,128]{1,0:T(8,128)(2,1)S(1)} %collective-permute-done) | copy-start | bytes 786436
  606.7 7.0 %collective-permute-start.1 = (bf16[1024,128]{1,0:T(8,128)(2,1)S(1)}, bf16[1024,128]{1,0:T(8,128)(2,1)S(1)}, u32[]{:S(2)}, u32[]{:S(2)}) collective-permute-start(bf16[1024,128]{1,0:T(8,128)(2,1)S(1)} %collective-permute-done), channel_id=1, source_target_pairs={{0,1},{1,2},{2,3},{3,4},{4,5},{5,6},{6,7},{7,0},{8,9},{9,10},{10,1... | collective-permute-start | bytes 786440 | tf_op jit(solution)/shard_map/ppermute | solution.py:161
  609.1 10.1 %collective-permute-start.4 = (bf16[1024,128]{1,0:T(8,128)(2,1)S(1)}, bf16[1024,128]{1,0:T(8,128)(2,1)}, u32[]{:S(2)}, u32[]{:S(2)}) collective-permute-start(bf16[1024,128]{1,0:T(8,128)(2,1)S(1)} %fusion.1), channel_id=1, source_target_pairs={{1,0},{2,1},{3,2},{4,3},{5,4},{6,5},{7,6},{0,7},{9,8},{10,9},{11,1... | collective-permute-start | bytes 786440 | tf_op jit(solution)/shard_map/ppermute | solution.py:164
  613.7 8.4 %collective-permute-start.2 = (bf16[1024,128]{1,0:T(8,128)(2,1)S(1)}, bf16[1024,128]{1,0:T(8,128)(2,1)}, u32[]{:S(2)}, u32[]{:S(2)}) collective-permute-start(bf16[1024,128]{1,0:T(8,128)(2,1)S(1)} %collective-permute-done.1), channel_id=1, source_target_pairs={{0,1},{1,2},{2,3},{3,4},{4,5},{5,6},{6,7},{7,0},{8,9},{9,10},{10,1... | collective-permute-start | bytes 786440 | tf_op jit(solution)/shard_map/ppermute | solution.py:161
  619.2 7.1 %collective-permute-start.5 = (bf16[1024,128]{1,0:T(8,128)(2,1)}, bf16[1024,128]{1,0:T(8,128)(2,1)S(1)}, u32[]{:S(2)}, u32[]{:S(2)}) collective-permute-start(bf16[1024,128]{1,0:T(8,128)(2,1)} %collective-permute-done.4), channel_id=1, source_target_pairs={{1,0},{2,1},{3,2},{4,3},{5,4},{6,5},{7,6},{0,7},{9,8},{10,9},{11,1... | collective-permute-start | bytes 786440 | tf_op jit(solution)/shard_map/ppermute | solution.py:164
  622.1 7.6 %collective-permute-start.3 = (bf16[1024,128]{1,0:T(8,128)(2,1)}, bf16[1024,128]{1,0:T(8,128)(2,1)S(1)}, u32[]{:S(2)}, u32[]{:S(2)}) collective-permute-start(bf16[1024,128]{1,0:T(8,128)(2,1)} %collective-permute-done.2), channel_id=1, source_target_pairs={{0,1},{1,2},{2,3},{3,4},{4,5},{5,6},{6,7},{7,0},{8,9},{9,10},{10,1... | collective-permute-start | bytes 786440 | tf_op jit(solution)/shard_map/ppermute | solution.py:161
  622.2 8.3 %copy-start.3 = (f32[8,128,4]{2,1,0:T(8,128)}, f32[8,128,4]{2,1,0:T(8,128)S(1)}, u32[]{:S(2)}) copy-start(f32[8,128,4]{2,1,0:T(8,128)S(1)} %broadcast_in_dim.112) | copy-start | bytes 49156
  622.2 10.0 %copy-start.12 = (bf16[1024,128]{1,0:T(8,128)(2,1)S(1)}, bf16[1024,128]{1,0:T(8,128)(2,1)}, u32[]{:S(2)}) copy-start(bf16[1024,128]{1,0:T(8,128)(2,1)} %copy-done.11) | copy-start | bytes 786436
  622.2 10.7 %copy-start.10 = (bf16[1024,128]{1,0:T(8,128)(2,1)S(1)}, bf16[1024,128]{1,0:T(8,128)(2,1)}, u32[]{:S(2)}) copy-start(bf16[1024,128]{1,0:T(8,128)(2,1)} %copy-done.9) | copy-start | bytes 786436
  626.3 10.4 %collective-permute-start.6 = (bf16[1024,128]{1,0:T(8,128)(2,1)S(1)}, bf16[1024,128]{1,0:T(8,128)(2,1)S(1)}, u32[]{:S(2)}, u32[]{:S(2)}) collective-permute-start(bf16[1024,128]{1,0:T(8,128)(2,1)S(1)} %collective-permute-done.5), channel_id=1, source_target_pairs={{1,0},{2,1},{3,2},{4,3},{5,4},{6,5},{7,6},{0,7},{9,8},{10,9},{11,1... | collective-permute-start | bytes 786440 | tf_op jit(solution)/shard_map/ppermute | solution.py:164
  646.5 35.1 %all-to-all-start.5 = ((bf16[32,32,512]{2,1,0:T(8,128)(2,1)}), bf16[32,32,512]{2,1,0:T(8,128)(2,1)S(1)}, u32[]{:S(2)}, u32[]{:S(2)}) async-start(bf16[32,32,512]{2,1,0:T(8,128)(2,1)} %bitcast.23), calls=%async_computation.5 | async-start | bytes 2097152 | tf_op jit(solution)/shard_map/all_to_all | solution.py:177
  667.6 14.1 %copy-start.20 = (s32[1024]{0:T(1024)S(1)}, s32[1024]{0:T(1024)}, u32[]{:S(2)}) copy-start(s32[1024]{0:T(1024)} %pad_clamp_fusion) | copy-start | bytes 12292
  (13 other events, 47.4 us)
